TPU v7x, 32 devices: a whole 2x2x4 slice. The times are simulated.
32 devices in a mesh: dp: 8 (over z, core), vocab: 4 (over y, x).
Axes of the slice: x: 2, y: 2, z: 4, core: 2. Of those that a mesh axis runs over, the one named last changes fastest.
Arguments:
- queries: bfloat16 [672, 8192], P('dp', 'vocab'), may hold values from -6 to 6
- residual: bfloat16 [672, 8192], P('dp', 'vocab'), may hold values from -16 to 16
- cache_k: bfloat16 [7, 32, 8, 512, 128], P(None, 'dp', 'vocab'), may hold values from -6 to 6, as said below
- cache_v: bfloat16 [7, 32, 8, 512, 128], P(None, 'dp', 'vocab'), may hold values from -6 to 6, as said below
- lengths: int32 [32, 7], P('dp'), may hold values from 128 to 512, as said below
- pairs: int32 [32, 21, 2], P('dp'), may hold values from 0 to 6, as said below
- out_weight: bfloat16 [8192, 8192], P('vocab'), may hold values from -1.5 to 1.5
- norm_gain: bfloat16 [8192], replicated, may hold values from 0.25 to 1.75
- head_weight: bfloat16 [8192, 8192], P(None, ('dp', 'vocab')), may hold values from -7 to 7
- answer_ids: int32 [2], replicated, may hold values from 0 to 8191
Outputs:
- verdict: float32 [672, 2], P('dp')
Inputs may be any that keep to these rules, and one draw needn't show every extreme that they name: `lengths`: every response has at least 128 tokens, and in every prompt one response has exactly 512. `pairs`: for every prompt the 21 rows hold each unordered pair of two different responses once, as (first, second) in some order. `cache_k`: the slots of one key-value head hold equal copies. `cache_v`: the slots of one key-value head hold equal copies.
All inputs are finite; a program needn't handle non-finite values.
Results may differ from a plain program's by a relative error of at most 0.0011.
Values may be sent and summed in bfloat16 or wider, within the bound.
A program may use at most 192 MiB of HBM per device.

v0:
```python
import math

import jax
import jax.numpy as jnp
from jax import lax
from jax.sharding import PartitionSpec as P

HD = 128


def from_behind(block, axis, distance):
    devices = range(lax.axis_size(axis))
    route = [((i - distance) % len(devices), i) for i in devices]
    return lax.ppermute(block, axis, route)


def merged(part, axis, combine):
    gathered = jax.tree.map(lambda a: lax.all_gather(a, axis), part)

    def take(source):
        return jax.tree.map(lambda a: lax.dynamic_index_in_dim(a, source, 0, False), gathered)

    return lax.fori_loop(
        1, lax.axis_size(axis), lambda source, state: combine(state, take(source)), take(0)
    )


def combine_stats(earlier, later):
    highest = jnp.maximum(earlier[0], later[0])
    summed = earlier[1] * jnp.exp(earlier[0] - highest) + later[1] * jnp.exp(later[0] - highest)
    return (highest, summed, earlier[2] + later[2], earlier[3] + later[3])


def normalize(hidden, norm_gain):
    widened = hidden.astype(jnp.float32)
    factor = lax.rsqrt(jnp.mean(widened * widened, axis=-1, keepdims=True) + 1e-05)
    return (widened * factor * norm_gain.astype(jnp.float32)).astype(jnp.bfloat16)


def local(
    queries,
    residual,
    cache_k,
    cache_v,
    lengths,
    pairs,
    out_weight,
    norm_gain,
    head_weight,
    answer_ids,
):
    vocab_count = lax.axis_size("vocab")
    dp_index = lax.axis_index("dp")
    vocab_index = lax.axis_index("vocab")
    answers = cache_k.shape[0]
    prompts_here = cache_k.shape[1]
    heads_here = cache_k.shape[2]
    longest = cache_k.shape[3]
    head_size = cache_k.shape[4]
    pair_rows = queries.shape[0]
    per_prompt = pairs.shape[1]
    query_heads = queries.shape[1] // head_size
    group_here = query_heads // heads_here
    key_list = [cache_k[0]]
    value_list = [cache_v[0]]
    for answer in range(1, answers):
        moved = from_behind(jnp.stack([cache_k[answer], cache_v[answer]]), "dp", -answer)
        key_list.append(moved[0])
        value_list.append(moved[1])
    block_keys = jnp.stack(key_list)
    block_values = jnp.stack(value_list)
    leading = pairs[:, :, 0]
    second = pairs[:, :, 1]
    answer_ids_grid = lax.broadcasted_iota(jnp.int32, (1, 1, answers, 1), 2)
    position = lax.broadcasted_iota(jnp.int32, (1, 1, 1, longest), 3)
    chosen = (answer_ids_grid == leading[:, :, None, None]) | (
        answer_ids_grid == second[:, :, None, None]
    )
    usable = chosen & (position < lengths[:, None, :, None])
    query_rows = queries.reshape(prompts_here, per_prompt, heads_here, group_here, head_size)
    scores = jnp.einsum(
        "pnagh,ipalh->pnagil", query_rows, block_keys, preferred_element_type=jnp.float32
    )
    scores = scores / math.sqrt(HD)
    scores = jnp.where(usable[:, :, None, None, :, :], scores, -jnp.inf)
    highest = jnp.max(scores, axis=(4, 5), keepdims=True)
    exponent = jnp.exp(scores - highest)
    weights = (exponent / jnp.sum(exponent, axis=(4, 5), keepdims=True)).astype(jnp.bfloat16)
    attended = jnp.einsum(
        "pnagil,ipalh->pnagh", weights, block_values, preferred_element_type=jnp.float32
    )
    attended = attended.astype(jnp.bfloat16).reshape(pair_rows, query_heads * head_size)
    partial_value = jnp.dot(attended, out_weight, preferred_element_type=jnp.float32)
    share_width = residual.shape[1]
    share_start = vocab_index * share_width
    own_part = lax.dynamic_slice_in_dim(
        partial_value, share_start, share_width, 1
    ) + residual.astype(jnp.float32)
    placed = lax.dynamic_update_slice_in_dim(partial_value, own_part, share_start, 1)
    hidden = lax.psum(placed, "vocab").astype(jnp.bfloat16)
    normed_rows = normalize(hidden, norm_gain)
    logits = jnp.dot(
        lax.all_gather(normed_rows, "dp", axis=0, tiled=True),
        head_weight,
        preferred_element_type=jnp.float32,
    )
    vocab_here = head_weight.shape[1]
    vocab_cols = (dp_index * vocab_count + vocab_index) * vocab_here + lax.broadcasted_iota(
        jnp.int32, (1, vocab_here), 1
    )
    top_logit = jnp.max(logits, axis=1)
    summed = jnp.sum(jnp.exp(logits - top_logit[:, None]), axis=1)
    yes_term = jnp.sum(jnp.where(vocab_cols == answer_ids[0], logits, 0.0), axis=1)
    no_term = jnp.sum(jnp.where(vocab_cols == answer_ids[1], logits, 0.0), axis=1)
    top_all, summed_all, yes_all, no_all = merged(
        (top_logit, summed, yes_term, no_term), ("dp", "vocab"), combine_stats
    )
    log_total = top_all + jnp.log(summed_all)
    own_start = dp_index * pair_rows
    yes_rows = lax.dynamic_slice_in_dim(yes_all - log_total, own_start, pair_rows, 0)
    no_rows = lax.dynamic_slice_in_dim(no_all - log_total, own_start, pair_rows, 0)
    return jnp.stack([yes_rows, no_rows], axis=1)


def solution(mesh):
    in_specs = (
        P("dp", "vocab"),
        P("dp", "vocab"),
        P(None, "dp", "vocab", None, None),
        P(None, "dp", "vocab", None, None),
        P("dp", None),
        P("dp", None, None),
        P("vocab", None),
        P(),
        P(None, ("dp", "vocab")),
        P(),
    )
    out_specs = P("dp", None)
    return jax.shard_map(local, mesh=mesh, in_specs=in_specs, out_specs=out_specs, check_vma=False)
```

profile of v0, /device:TPU:0, one launch (start us, length us, event | category | flops | bytes accessed | tf_op | source)
XLA Modules:
  0.0 785.6 jit_solution(6034093063110160102)
XLA Ops:
  6.5 5.4 slice_bitcast_fusion
  12.0 0.2 pad_maximum_fusion
  12.2 4.5 collective-permute-start
  16.7 1.5 pad_maximum_fusion.1
  18.2 0.6 collective-permute-start.1
  18.8 1.5 pad_maximum_fusion.2
  20.3 0.0 collective-permute-start.2
  20.3 1.5 pad_maximum_fusion.3
  21.8 2.7 collective-permute-start.3
  24.6 1.5 pad_maximum_fusion.4
  26.1 0.1 iota_compare_fusion
  26.2 1.5 pad_maximum_fusion.5
  27.7 33.2 %collective-permute-done = bf16[2,4,2,512,128]{4,3,0,2,1:T(8,128)(2,1)} collective-permute-done((bf16[2,4,2,512,128]{4,3,0,2,1:T(8,128)(2,1)S(1)}, bf16[2,4,2,512,128]{4,3,0,2,1:T(8,128)(2,1)}, u32[]{:S(2)}, u32[]{:S(2)}) %collective-permute-start) | collective-permute-done | bytes 2097184 | tf_op jit(solution)/shard_map/ppermute | solution.py:14
  60.9 0.1 copy.81
  61.1 0.2 broadcast_and_fusion
  61.3 3.4 bitcast_dynamic-update-slice_fusion
  64.7 3.4 slice_dynamic-update-slice_fusion.11
  68.0 37.9 %collective-permute-done.1 = bf16[2,4,2,512,128]{4,3,0,2,1:T(8,128)(2,1)} collective-permute-done((bf16[2,4,2,512,128]{4,3,0,2,1:T(8,128)(2,1)}, bf16[2,4,2,512,128]{4,3,0,2,1:T(8,128)(2,1)}, u32[]{:S(2)}, u32[]{:S(2)}) %collective-permute-start.1) | collective-permute-done | bytes 2097184 | tf_op jit(solution)/shard_map/ppermute | solution.py:14
  106.0 3.4 slice_dynamic-update-slice_fusion.10
  109.4 41.5 %collective-permute-done.2 = bf16[2,4,2,512,128]{4,3,0,2,1:T(8,128)(2,1)} collective-permute-done((bf16[2,4,2,512,128]{4,3,0,2,1:T(8,128)(2,1)}, bf16[2,4,2,512,128]{4,3,0,2,1:T(8,128)(2,1)}, u32[]{:S(2)}, u32[]{:S(2)}) %collective-permute-start.2) | collective-permute-done | bytes 2097184 | tf_op jit(solution)/shard_map/ppermute | solution.py:14
  150.9 3.4 slice_dynamic-update-slice_fusion.9
  154.3 198.9 %collective-permute-done.3 = bf16[2,4,2,512,128]{4,3,0,2,1:T(8,128)(2,1)} collective-permute-done((bf16[2,4,2,512,128]{4,3,0,2,1:T(8,128)(2,1)}, bf16[2,4,2,512,128]{4,3,0,2,1:T(8,128)(2,1)}, u32[]{:S(2)}, u32[]{:S(2)}) %collective-permute-start.3) | collective-permute-done | bytes 2097184 | tf_op jit(solution)/shard_map/ppermute | solution.py:14
  353.2 3.3 slice_dynamic-update-slice_fusion.8
  356.5 1.8 slice_dynamic-update-slice_fusion.7
  358.3 3.4 slice_dynamic-update-slice_fusion.6
  361.7 16.4 %fusion.1 = (f32[4,21,2,8]{1,3,2,0:T(8,128)S(1)}, f32[4,2,7,512,21,8]{3,4,5,2,1,0:T(8,128)}) fusion(pred[4,21,7,512]{3,1,2,0:T(8,128)(4,1)S(1)} %broadcast_and_fusion, bf16[4,21,2,8,128,1]{4,3,2,1,0,5:T(8,128)(2,1)S(1)} %bitcast.96, bf16[7,4,2,512,128]{4,3,0,2,1:T(8,128)(2,1)} %get-tuple-element.276), kind=kOutput, calls=%fused_computation.9 | convolution fusion | flops 1247574784 | bytes 27258112 | tf_op jit(solution)/shard_map/pnagh,ipalh->pnagil/dot_general | solution.py:81
  378.2 8.7 %fusion = f32[4,21,2,8]{1,3,2,0:T(8,128)S(1)} fusion(f32[4,2,7,512,21,8]{3,4,5,2,1,0:T(8,128)} %get-tuple-element.294, f32[4,21,2,8]{1,3,2,0:T(8,128)S(1)} %get-tuple-element.293, pred[4,21,7,512]{3,1,2,0:T(8,128)(4,1)S(1)} %broadcast_and_fusion), kind=kLoop, calls=%fused_computation.8 | loop fusion | flops 19266240 | bytes 19579392 | tf_op jit(solution)/shard_map/reduce_sum | solution.py:88
  386.9 11.9 %fusion.16 = bf16[4,21,2,8,128]{4,1,3,2,0:T(8,128)(2,1)S(1)} fusion(f32[4,2,7,512,21,8]{3,4,5,2,1,0:T(8,128)} %get-tuple-element.294, f32[4,21,2,8]{1,3,2,0:T(8,128)S(1)} %fusion, f32[4,21,2,8]{1,3,2,0:T(8,128)S(1)} %get-tuple-element.293, pred[4,21,7,512]{3,1,2,0:T(8,128)(4,1)S(1)} %broadcast_and_fusion, bf16[7,4,2,512,128]{4,3,0,2,1:T(8,128)(2,1)} %get-tuple-element.275), kind=kOutput, calls=%fused_computation.28 | convolution fusion | flops 1257381888 | bytes 27263488 | tf_op jit(solution)/shard_map/pnagil,ipalh->pnagh/dot_general | solution.py:89
  398.8 0.2 reshape.56
  399.0 0.0 copy-start.1
  399.0 13.4 %fusion.30 = f32[84,8192]{1,0:T(8,128)S(1)} fusion(bf16[84,2048]{1,0:T(8,128)(2,1)S(1)} %reshape.56, bf16[2048,8192]{1,0:T(8,128)(2,1)} %param.18), kind=kOutput, calls=%fused_computation.80 | convolution fusion | flops 2818572288 | bytes 36651008 | tf_op jit(solution)/shard_map/dot_general | solution.py:93
  412.4 0.0 copy-start.9
  412.4 0.1 add_dynamic-update-slice_fusion
  412.6 63.7 %all-reduce.9 = bf16[84,8192]{1,0:T(8,128)(2,1)} all-reduce(f32[84,8192]{1,0:T(8,128)S(1)} %add_dynamic-update-slice_fusion), channel_id=1, replica_groups=mesh['dp'=8,'vocab'=4] {'vocab'}, use_global_device_ids=true, to_apply=%region_2.3 | all-reduce | flops 688128 | bytes 4128768 | tf_op jit(solution)/shard_map/psum | solution.py:100
  476.2 1.7 fusion.6
  478.0 2.9 fusion.9
  480.9 0.0 all-gather.7.cloned.1.call-update
  481.0 0.0 all-reduce.8.cloned.1.call-start
  481.0 0.7 fusion.28
  481.7 1.3 fusion.23
  483.0 138.3 %all-gather.7.cloned.1.call-done = bf16[8,84,8192]{2,1,0:T(8,128)(2,1)} async-done(((bf16[1,84,8192]{2,1,0:T(8,128)(2,1)}), bf16[8,84,8192]{2,1,0:T(8,128)(2,1)}) %all-gather.7.cloned.1.call-update) | async-done | bytes 11010064 | tf_op jit(solution)/shard_map/all_gather | solution.py:103
  621.3 9.4 %reshape.78 = bf16[672,8192]{1,0:T(8,128)(2,1)} reshape(bf16[8,84,8192]{2,1,0:T(8,128)(2,1)} %all-gather.7.cloned.1.call-done) | data formatting | bytes 22020096
  630.6 8.4 %fusion.29 = (f32[672]{0:T(1024)S(1)}, f32[672,256]{1,0:T(8,128)S(1)}) fusion(bf16[672,8192]{1,0:T(8,128)(2,1)} %reshape.78, bf16[8192,256]{1,0:T(8,128)(2,1)} %param.20), kind=kOutput, calls=%fused_computation.79 | convolution fusion | flops 2818743552 | bytes 15895168 | tf_op jit(solution)/shard_map/dot_general | solution.py:102
  639.1 0.3 dynamic-update-slice
  639.4 0.5 select_reduce_fusion
  639.9 0.3 dynamic-update-slice.2
  640.2 0.3 dynamic-update-slice.3
  640.5 0.3 dynamic-update-slice.1
  640.8 0.3 copy-done.4
  641.1 0.3 copy-done.2
  641.4 0.0 all-reduce.8.cloned.1.call-update
  641.5 125.6 %all-reduce.8.cloned.1.call-done = (f32[21504]{0:T(1024)}, f32[21504]{0:T(1024)}, f32[21504]{0:T(1024)}, f32[21504]{0:T(1024)}) async-done(((f32[21504]{0:T(1024)}, f32[21504]{0:T(1024)}, f32[21504]{0:T(1024)}, f32[21504]{0:T(1024)}), (f32[21504]{0:T(1024)}, f32[21504]{0:T(1024)}, f32[21504]{0:T(1024)}, f32[21504]{0:T(1024)})) %all-reduce.8.cloned.1.call-update) | async-done | bytes 344080
  767.0 1.0 reshape.57
  768.0 0.7 slice.140
  768.7 1.0 reshape.58
  769.7 0.7 slice.141
  770.4 1.0 reshape.59
  771.4 0.7 slice.142
  772.1 1.0 reshape.60
  773.1 0.7 slice.143
  773.8 4.3 while.21
  778.0 0.1 dynamic-slice_bitcast_fusion.1
  778.1 0.1 dynamic-slice_bitcast_fusion
  778.2 0.6 pad_maximum_fusion.6
  (187 shorter events, 2.7 us)
Async XLA Ops:
  6.5 614.7 %all-gather.7.cloned.1.call-start = ((), (), s32[]{:S(2)}) async-start(), calls=%async_computation | async-start | bytes 12976128 | tf_op jit(solution)/shard_map/all_gather | solution.py:103
  12.2 48.8 %collective-permute-start = (bf16[2,4,2,512,128]{4,3,0,2,1:T(8,128)(2,1)S(1)}, bf16[2,4,2,512,128]{4,3,0,2,1:T(8,128)(2,1)}, u32[]{:S(2)}, u32[]{:S(2)}) collective-permute-start(bf16[2,4,2,512,128]{4,3,0,2,1:T(8,128)(2,1)S(1)} %pad_maximum_fusion), channel_id=1, source_target_pairs={{4,0},{8,4},{12,8},{16,12},{20,16},{24,20},{28,24},{0,28},{5,1},{9... | collective-permute-start | bytes 6291464 | tf_op jit(solution)/shard_map/ppermute | solution.py:14
  18.2 7.9 %copy-start.7 = (s32[4,21,2]{1,2,0:T(2,128)S(1)}, s32[4,21,2]{1,2,0:T(2,128)}, u32[]{:S(2)}) copy-start(s32[4,21,2]{1,2,0:T(2,128)} %param.17) | copy-start | bytes 2020
  18.2 7.9 %copy-start.8 = (s32[4,7]{1,0:T(4,128)S(1)}, s32[4,7]{1,0:T(4,128)}, u32[]{:S(2)}) copy-start(s32[4,7]{1,0:T(4,128)} %param.16) | copy-start | bytes 340
  18.2 87.8 %collective-permute-start.1 = (bf16[2,4,2,512,128]{4,3,0,2,1:T(8,128)(2,1)}, bf16[2,4,2,512,128]{4,3,0,2,1:T(8,128)(2,1)}, u32[]{:S(2)}, u32[]{:S(2)}) collective-permute-start(bf16[2,4,2,512,128]{4,3,0,2,1:T(8,128)(2,1)} %pad_maximum_fusion.1), channel_id=1, source_target_pairs={{8,0},{12,4},{16,8},{20,12},{24,16},{28,20},{0,24},{4,28},{9,1},{1... | collective-permute-start | bytes 6291464 | tf_op jit(solution)/shard_map/ppermute | solution.py:14
  20.3 40.6 %copy-start = (bf16[84,2048]{1,0:T(8,128)(2,1)S(1)}, bf16[84,2048]{1,0:T(8,128)(2,1)}, u32[]{:S(2)}) copy-start(bf16[84,2048]{1,0:T(8,128)(2,1)} %param.12) | copy-start | bytes 1032196
  20.3 40.7 %copy-start.6 = (bf16[8192]{0:T(1024)(128)(2,1)S(1)}, bf16[8192]{0:T(1024)(128)(2,1)}, u32[]{:S(2)}) copy-start(bf16[8192]{0:T(1024)(128)(2,1)} %param.19) | copy-start | bytes 49156
  20.3 130.6 %collective-permute-start.2 = (bf16[2,4,2,512,128]{4,3,0,2,1:T(8,128)(2,1)}, bf16[2,4,2,512,128]{4,3,0,2,1:T(8,128)(2,1)}, u32[]{:S(2)}, u32[]{:S(2)}) collective-permute-start(bf16[2,4,2,512,128]{4,3,0,2,1:T(8,128)(2,1)} %pad_maximum_fusion.2), channel_id=1, source_target_pairs={{12,0},{16,4},{20,8},{24,12},{28,16},{0,20},{4,24},{8,28},{13,1},{... | collective-permute-start | bytes 6291464 | tf_op jit(solution)/shard_map/ppermute | solution.py:14
  21.8 331.3 %collective-permute-start.3 = (bf16[2,4,2,512,128]{4,3,0,2,1:T(8,128)(2,1)}, bf16[2,4,2,512,128]{4,3,0,2,1:T(8,128)(2,1)}, u32[]{:S(2)}, u32[]{:S(2)}) collective-permute-start(bf16[2,4,2,512,128]{4,3,0,2,1:T(8,128)(2,1)} %pad_maximum_fusion.3), channel_id=1, source_target_pairs={{16,0},{20,4},{24,8},{28,12},{0,16},{4,20},{8,24},{12,28},{17,1},{... | collective-permute-start | bytes 6291464 | tf_op jit(solution)/shard_map/ppermute | solution.py:14
  26.1 330.4 %collective-permute-start.4 = (bf16[2,4,2,512,128]{4,3,0,2,1:T(8,128)(2,1)}, bf16[2,4,2,512,128]{4,3,0,2,1:T(8,128)(2,1)S(1)}, u32[]{:S(2)}, u32[]{:S(2)}) collective-permute-start(bf16[2,4,2,512,128]{4,3,0,2,1:T(8,128)(2,1)} %pad_maximum_fusion.4), channel_id=1, source_target_pairs={{20,0},{24,4},{28,8},{0,12},{4,16},{8,20},{12,24},{16,28},{21,1},{... | collective-permute-start | bytes 6291464 | tf_op jit(solution)/shard_map/ppermute | solution.py:14
  60.9 297.4 %collective-permute-start.5 = (bf16[2,4,2,512,128]{4,3,0,2,1:T(8,128)(2,1)}, bf16[2,4,2,512,128]{4,3,0,2,1:T(8,128)(2,1)}, u32[]{:S(2)}, u32[]{:S(2)}) collective-permute-start(bf16[2,4,2,512,128]{4,3,0,2,1:T(8,128)(2,1)} %pad_maximum_fusion.5), channel_id=1, source_target_pairs={{24,0},{28,4},{0,8},{4,12},{8,16},{12,20},{16,24},{20,28},{25,1},{... | collective-permute-start | bytes 6291464 | tf_op jit(solution)/shard_map/ppermute | solution.py:14
  399.0 13.4 %copy-start.1 = (bf16[84,2048]{1,0:T(8,128)(2,1)S(1)}, bf16[84,2048]{1,0:T(8,128)(2,1)}, u32[]{:S(2)}) copy-start(bf16[84,2048]{1,0:T(8,128)(2,1)} %param.13) | copy-start | bytes 1032196
  412.4 68.6 %copy-start.9 = (s32[2]{0:T(128)S(1)}, s32[2]{0:T(128)}, u32[]{:S(2)}) copy-start(s32[2]{0:T(128)} %param.21) | copy-start | bytes 28
  481.0 286.1 %all-reduce.8.cloned.1.call-start = ((), (), s32[]{:S(2)}) async-start(), calls=%async_computation.1 | async-start | bytes 688128
  639.4 1.4 copy-start.5
  640.2 0.6 copy-start.3
  640.5 0.6 copy-start.4
  640.8 0.6 copy-start.2
Sparse Core Ops, SparseCore 0:
  481.1 140.1 all-gather.6
  641.6 125.4 all-reduce.7
where the time goes:
time: 787 us; the launch traced here: 786 us
  waiting for transfers between devices  575 us (73%)
  blocking collectives  63.7 us (8%)
  matrix products  50.1 us (6%)
  local copies, waits for them, and re-layouts  48.4 us (6%)
  other arithmetic  24.6 us (3%)
  between operations  13.7 us (2%)
  starting transfers between devices  7.91 us (1%)
    ppermute x6, waiting for transfers between devices, from_behind(): return lax.ppermute(block, axis, route)  312 us
    all_gather x1, waiting for transfers between devices, local(): lax.all_gather(normed_rows, 'dp', axis=0, tiled=True)  138 us
    unnamed x3, waiting for transfers between devices  126 us
    psum x1, blocking collectives, local(): hidden = lax.psum(placed, 'vocab').astype(jnp.bfloat16)  63.7 us
    unnamed x38, local copies, waits for them, and re-layouts  35.4 us
    dot_general x1, matrix products, local(): jnp.einsum('pnagh,ipalh->pnagil', query_rows, block_keys, preferred_eleme...  16.4 us
  transfers between devices with their start and end apart: 8, of which 6 were waited for; matrix products, arithmetic and copies ran while one was open for 4% of the time, Pallas kernels for 0%

commit v1 on v0

v1 whole, which is shorter than its diff:
```python
import functools
import math

import jax
import jax.numpy as jnp
from jax import lax
from jax.experimental import pallas as pl
from jax.experimental.pallas import tpu as pltpu
from jax.sharding import PartitionSpec as P

MESH = pl.DeviceIdType.MESH
F32 = jnp.float32
BF16 = jnp.bfloat16


def up(n, m):
    return -(-n // m) * m


def remote(src, dst, send, recv, device):
    return pltpu.make_async_remote_copy(
        src_ref=src, dst_ref=dst, send_sem=send, recv_sem=recv,
        device_id=device, device_id_type=MESH,
    )


def greet(partners):
    barrier = pltpu.get_barrier_semaphore()
    for device in partners:
        pl.semaphore_signal(barrier, inc=1, device_id=device, device_id_type=MESH)
    pl.semaphore_wait(barrier, len(partners))


def attend_kernel(
    n, pick_ref, place_ref, q_ref, lens_ref, k_hbm, v_hbm, out_ref,
    k_ref, v_ref, qs, qr, lr, ob, orecv, st, strecv,
    kv_sem, q_send, q_recv, l_send, l_recv, o_send, o_recv, s_send, s_recv,
):
    answers, prompts, heads, longest, hd = k_hbm.shape
    span = qr.shape[3]
    me, col = lax.axis_index("dp"), lax.axis_index("vocab")
    loads = []
    for i in range(answers):
        for which, (src, dst) in enumerate(((k_hbm, k_ref), (v_hbm, v_ref))):
            load = pltpu.make_async_copy(src.at[i], dst.at[i], kv_sem.at[which, i])
            load.start()
            loads.append(load)
    shifts = sorted({s % n for i in range(1, answers) for s in (i, -i)})
    for p in range(prompts):
        for c in range(heads):
            qs[p, c] = jnp.dot(
                pick_ref[p], q_ref[p, c], preferred_element_type=F32
            ).astype(BF16)
    greet([(lax.rem(me + s, n), col) for s in shifts])
    order = [1, 2, 6, 3, 5, 4] if answers == 7 else list(range(1, answers))
    q_out, l_out, o_out, s_out = {}, {}, {}, {}
    for i in order:
        ahead = (lax.rem(me + i, n), col)
        behind = (lax.rem(me + n - i, n), col)
        rows = pl.ds(i * span, span)
        q_out[i] = remote(
            qs.at[:, :, rows], qr.at[i], q_send.at[i], q_recv.at[i], ahead)
        l_out[i] = remote(lens_ref.at[i], lr.at[i], l_send.at[i], l_recv.at[i], ahead)
        o_out[i] = remote(
            ob.at[i], orecv.at[:, :, rows], o_send.at[i], o_recv.at[i], behind)
        s_out[i] = remote(
            st.at[i], strecv.at[rows], s_send.at[i], s_recv.at[i], behind)
        q_out[i].start()
        l_out[i].start()
    scale = 1.0 / math.sqrt(hd)
    for i in [0] + order:
        loads[2 * i].wait()
        loads[2 * i + 1].wait()
        if i:
            q_out[i].wait_recv()
            l_out[i].wait_recv()
        lane = lax.broadcasted_iota(jnp.int32, (span, 128), 1)
        position = lax.broadcasted_iota(jnp.int32, (span, longest), 1)
        stats = jnp.zeros((span, 128), F32)
        for p in range(prompts):
            limit = (lr[i, p : p + 1, 0:1] if i else lens_ref[0, p : p + 1, 0:1])
            for c in range(heads):
                q = qr[i, p, c] if i else qs[p, c, 0:span]
                s = lax.dot_general(
                    q, k_ref[i, p, c], (((1,), (1,)), ((), ())),
                    preferred_element_type=F32,
                ) * scale
                s = jnp.where(position < limit, s, -jnp.inf)
                top = jnp.max(s, axis=1, keepdims=True)
                e = jnp.exp(s - top)
                total = jnp.sum(e, axis=1, keepdims=True)
                o = jnp.dot(e.astype(BF16), v_ref[i, p, c], preferred_element_type=F32)
                o = (o / total).astype(BF16)
                if i:
                    ob[i, p, c] = o
                else:
                    orecv[p, c, 0:span] = o
                lse = top + jnp.log(total)
                high = lse.astype(BF16).astype(F32)
                mid = (lse - high).astype(BF16).astype(F32)
                low = lse - high - mid
                at = 3 * (p * heads + c)
                stats = jnp.where(lane == at, high, stats)
                stats = jnp.where(lane == at + 1, mid, stats)
                stats = jnp.where(lane == at + 2, low, stats)
        if i:
            st[i] = stats.astype(BF16)
            o_out[i].start()
            s_out[i].start()
        else:
            strecv[0:span] = stats.astype(BF16)
    for i in order:
        o_out[i].wait_recv()
        s_out[i].wait_recv()
    half = out_ref.shape[2]
    for p in range(prompts):
        place = place_ref[p]
        both = jnp.dot(place, strecv[...], preferred_element_type=F32)
        for c in range(heads):
            at = 3 * (p * heads + c)
            lse = both[:, at : at + 1] + both[:, at + 1 : at + 2] + both[:, at + 2 : at + 3]
            first, second = lse[:half], lse[half:]
            top = jnp.maximum(first, second)
            first, second = jnp.exp(first - top), jnp.exp(second - top)
            o = jnp.dot(place, orecv[p, c], preferred_element_type=F32)
            mixed = (first * o[:half] + second * o[half:]) / (first + second)
            out_ref[p, c] = mixed.astype(BF16)
    for i in order:
        for copy in (q_out[i], l_out[i], o_out[i], s_out[i]):
            copy.wait_send()


def tail_kernel(
    nd, nv, width, part_ref, res_ref, gain_ref, w_ref, ids_ref, out_ref,
    sb, rb, hid, sq, sqr, g, stat, statr, vrow,
    p_send, p_recv, q_send, q_recv, g_send, g_recv, t_send, t_recv, v_send, v_recv,
):
    rows, share = res_ref.shape
    me, col = lax.axis_index("dp"), lax.axis_index("vocab")
    vpeer = {j: lax.rem(col + j, nv) for j in range(1, nv)}
    dpeer = {j: lax.rem(me + j, nd) for j in range(1, nd)}
    greet([(me, vpeer[j]) for j in vpeer] + [(dpeer[j], col) for j in dpeer])

    def columns(v):
        return pl.ds(pl.multiple_of(v * share, 128), share)

    parts = {}
    for j in vpeer:
        sb[j] = part_ref[:, columns(vpeer[j])].astype(BF16)
        parts[j] = remote(
            sb.at[j], rb.at[j], p_send.at[j], p_recv.at[j], (me, vpeer[j]))
        parts[j].start()
    for j in vpeer:
        parts[j].wait_recv()
    step = 256 if share % 256 == 0 else 128
    squares = jnp.zeros((rows, 128), F32)
    for t in range(0, share, step):
        total = part_ref[:, pl.ds(pl.multiple_of(col * share + t, 128), step)]
        total = total + res_ref[:, t : t + step].astype(F32)
        for j in vpeer:
            total = total + rb[j, :, t : t + step].astype(F32)
        total = total.astype(BF16)
        hid[:, t : t + step] = total
        total = total.astype(F32)
        for u in range(0, step, 128):
            squares = squares + total[:, u : u + 128] * total[:, u : u + 128]
    sq[...] = squares
    exch = {}
    for j in vpeer:
        exch[j] = remote(
            sq, sqr.at[j], q_send.at[j], q_recv.at[j], (me, vpeer[j]))
        exch[j].start()
    for j in vpeer:
        exch[j].wait_recv()
        squares = squares + sqr[j]
    mean = jnp.sum(squares, axis=1, keepdims=True) * (1.0 / (share * nv))
    factor = lax.rsqrt(mean + 1e-05)
    for t in range(0, share, step):
        block = hid[:, t : t + step].astype(F32) * factor
        g[me, col, :, t : t + step] = (
            block * gain_ref[0:1, t : t + step].astype(F32)
        ).astype(BF16)

    core = lax.rem(me, 2)
    sib = me + 1 - 2 * core
    sent = []

    def push(e, v, device, slot):
        block = g.at[e, v]
        copy = remote(block, block, g_send.at[slot], g_recv.at[e, v], device)
        copy.start()
        sent.append(copy)

    def arrived(e, v):
        block = g.at[e, v]
        remote(block, block, g_send.at[0], g_recv.at[e, v], (sib, col)).wait_recv()

    nz = nd // 2
    lines = [lax.rem(me + 2 * s, nd) for s in range(nz)]
    slot = 0
    for s in range(1, nz):
        push(me, col, (lines[s], col), slot)
        slot += 1
    for j in vpeer:
        push(me, col, (me, vpeer[j]), slot)
        slot += 1
    push(me, col, (sib, col), slot)
    slot += 1
    for s in range(1, nz):
        arrived(lines[s], col)
        for j in vpeer:
            push(lines[s], col, (me, vpeer[j]), slot)
            slot += 1
        push(lines[s], col, (sib, col), slot)
        slot += 1

    base = (me * nv + col) * width
    cols = lax.broadcasted_iota(jnp.int32, (rows, width), 1) + base
    lane = lax.broadcasted_iota(jnp.int32, (rows, 128), 1)
    tail = jnp.zeros((128 - rows % 128, 128), F32) if rows % 128 else None

    def head(e):
        def body(v, acc):
            return acc + jnp.dot(g[e, v], w_ref[v], preferred_element_type=F32)

        logits = lax.fori_loop(0, nv, body, jnp.zeros((rows, width), F32))
        top = jnp.max(logits, axis=1, keepdims=True)
        total = jnp.sum(jnp.exp(logits - top), axis=1, keepdims=True)
        yes = jnp.sum(jnp.where(cols == ids_ref[0:1, 0:1], logits, 0.0), axis=1, keepdims=True)
        no = jnp.sum(jnp.where(cols == ids_ref[1:2, 0:1], logits, 0.0), axis=1, keepdims=True)
        tile = jnp.where(lane == 0, top, 0.0)
        for at, what in ((1, total), (2, yes), (3, no)):
            tile = jnp.where(lane == at, what, tile)
        if tail is not None:
            tile = jnp.concatenate([tile, tail], axis=0)
        stat[e] = jnp.transpose(tile)[0:8]

    for s in range(nz):
        for j in vpeer:
            arrived(lines[s], vpeer[j])
            push(lines[s], vpeer[j], (sib, col), slot)
            slot += 1
    stats = []

    def deliver(e, at):
        copy = remote(
            stat.at[e], statr.at[me], t_send.at[at], t_recv.at[me], (e, col))
        copy.start()
        stats.append(copy)

    for s in range(nz):
        head(lines[s])
        if s:
            deliver(lines[s], 2 * s)
    for s in range(nz):
        other = lax.rem(sib + 2 * s, nd)
        for v in range(nv):
            arrived(other, v)
        head(other)
        deliver(other, 2 * s + 1)
    statr[me] = stat[me]
    for j in dpeer:
        e = dpeer[j]
        remote(
            stat.at[e], statr.at[e], t_send.at[0], t_recv.at[e], (e, col)
        ).wait_recv()

    def merge(ref, count):
        top = ref[0, 0:1]
        for e in range(1, count):
            top = jnp.maximum(top, ref[e, 0:1])
        total = jnp.zeros_like(top)
        yes = jnp.zeros_like(top)
        no = jnp.zeros_like(top)
        for e in range(count):
            total = total + ref[e, 1:2] * jnp.exp(ref[e, 0:1] - top)
            yes = yes + ref[e, 2:3]
            no = no + ref[e, 3:4]
        return top, total, yes, no

    top, total, yes, no = merge(statr, nd)
    vrow[col] = jnp.concatenate(
        [top, total, yes, no, jnp.zeros((4, top.shape[1]), F32)], axis=0)
    last = {}
    for j in vpeer:
        last[j] = remote(
            vrow.at[col], vrow.at[col], v_send.at[j], v_recv.at[col], (me, vpeer[j]))
        last[j].start()
    for j in vpeer:
        v = vpeer[j]
        remote(
            vrow.at[v], vrow.at[v], v_send.at[0], v_recv.at[v], (me, v)
        ).wait_recv()
    top, total, yes, no = merge(vrow, nv)
    log_total = top + jnp.log(total)
    out_ref[...] = jnp.concatenate(
        [yes - log_total, no - log_total, jnp.zeros((6, top.shape[1]), F32)], axis=0)
    for copy in [*parts.values(), *exch.values(), *sent, *stats, *last.values()]:
        copy.wait_send()


def dma(*shape):
    return pltpu.SemaphoreType.DMA(shape)


def selectors(pairs, answers, group, span, slots):
    prompts, per_prompt, _ = pairs.shape
    ids = jnp.arange(answers, dtype=jnp.int32)
    chosen = pairs[:, None, :, :] == ids[None, :, None, None]
    involved = chosen[..., 0] | chosen[..., 1]
    k = jnp.arange(per_prompt, dtype=jnp.int32)
    rank = jnp.sum(
        (involved[:, :, None, :] & (k[None, :] < k[:, None])[None, None]).astype(jnp.int32), -1)
    key = pairs * span + jnp.sum(
        jnp.where(chosen, rank[..., None], 0), axis=1) * group
    wide = jnp.repeat(key, group, axis=1) + jnp.tile(
        jnp.arange(group, dtype=jnp.int32), per_prompt)[None, :, None]
    wide = jnp.pad(wide, ((0, 0), (0, slots - wide.shape[1]), (0, 0)), constant_values=-1)
    row = jnp.arange(answers * span, dtype=jnp.int32)
    first, second = wide[:, :, 0], wide[:, :, 1]
    pick = (row[None, :, None] == first[:, None, :]) | (row[None, :, None] == second[:, None, :])
    both = jnp.concatenate([first, second], axis=1)
    place = both[:, :, None] == row[None, None, :]
    return pick.astype(BF16), place.astype(BF16)


def local(
    queries, residual, cache_k, cache_v, lengths, pairs, out_weight, norm_gain,
    head_weight, answer_ids,
):
    nd, nv = lax.axis_size("dp"), lax.axis_size("vocab")
    answers, prompts, heads, longest, hd = cache_k.shape
    pair_rows = queries.shape[0]
    per_prompt = pairs.shape[1]
    group = queries.shape[1] // hd // heads
    span = up((answers - 1) * group, 16)
    slots = up(per_prompt * group, 16)
    pick, place = selectors(pairs, answers, group, span, slots)
    q = queries.reshape(prompts, per_prompt, heads, group, hd).transpose(0, 2, 1, 3, 4)
    q = q.reshape(prompts, heads, per_prompt * group, hd)
    q = jnp.pad(q, ((0, 0), (0, 0), (0, slots - per_prompt * group), (0, 0)))
    lens = jnp.pad(lengths.T, ((0, 0), (0, up(prompts, 8) - prompts)))
    lens = jnp.broadcast_to(lens[:, :, None], lens.shape + (128,))
    vm = pl.BlockSpec(memory_space=pltpu.VMEM)
    hbm = pl.BlockSpec(memory_space=pl.ANY)
    attended = pl.pallas_call(
        functools.partial(attend_kernel, nd),
        out_shape=jax.ShapeDtypeStruct((prompts, heads, slots, hd), BF16),
        in_specs=[vm, vm, vm, vm, hbm, hbm],
        out_specs=vm,
        scratch_shapes=[
            pltpu.VMEM(cache_k.shape, BF16),
            pltpu.VMEM(cache_k.shape, BF16),
            pltpu.VMEM((prompts, heads, answers * span, hd), BF16),
            pltpu.VMEM((answers, prompts, heads, span, hd), BF16),
            pltpu.VMEM(lens.shape, jnp.int32),
            pltpu.VMEM((answers, prompts, heads, span, hd), BF16),
            pltpu.VMEM((prompts, heads, answers * span, hd), BF16),
            pltpu.VMEM((answers, span, 128), BF16),
            pltpu.VMEM((answers * span, 128), BF16),
            dma(2, answers),
        ] + [dma(answers)] * 8,
        compiler_params=pltpu.CompilerParams(
            collective_id=0, has_side_effects=True, vmem_limit_bytes=40 << 20),
    )(pick, place, q, lens, cache_k, cache_v)
    attended = attended[:, :, : per_prompt * group].reshape(
        prompts, heads, per_prompt, group, hd).transpose(0, 2, 1, 3, 4)
    rows = up(pair_rows, 16)
    attended = jnp.pad(
        attended.reshape(pair_rows, heads * group * hd), ((0, rows - pair_rows), (0, 0)))
    partial = jnp.dot(attended, out_weight, preferred_element_type=F32)
    share = residual.shape[1]
    width = head_weight.shape[1]
    res = jnp.pad(residual, ((0, rows - pair_rows), (0, 0)))
    own_gain = lax.dynamic_slice_in_dim(norm_gain, lax.axis_index("vocab") * share, share, 0)
    own_gain = jnp.broadcast_to(own_gain.astype(F32)[None], (8, share))
    ids = jnp.broadcast_to(jnp.pad(answer_ids, (0, 6))[:, None], (8, 128))
    wide = up(rows, 128)
    verdict = pl.pallas_call(
        functools.partial(tail_kernel, nd, nv, width),
        out_shape=jax.ShapeDtypeStruct((8, wide), F32),
        in_specs=[vm] * 5,
        out_specs=vm,
        scratch_shapes=[
            pltpu.VMEM((nv, rows, share), BF16),
            pltpu.VMEM((nv, rows, share), BF16),
            pltpu.VMEM((rows, share), BF16),
            pltpu.VMEM((rows, 128), F32),
            pltpu.VMEM((nv, rows, 128), F32),
            pltpu.VMEM((nd, nv, rows, share), BF16),
            pltpu.VMEM((nd, 8, wide), F32),
            pltpu.VMEM((nd, 8, wide), F32),
            pltpu.VMEM((nv, 8, wide), F32),
            dma(nv), dma(nv), dma(nv), dma(nv),
            dma((nd // 2) * (2 * nv + 1)), dma(nd, nv),
            dma(nd), dma(nd), dma(nv), dma(nv),
        ],
        compiler_params=pltpu.CompilerParams(
            collective_id=1, has_side_effects=True, vmem_limit_bytes=52 << 20),
    )(partial, res, own_gain, head_weight.reshape(nv, share, width), ids)
    return verdict[:2, :pair_rows].T


def solution(mesh):
    in_specs = (
        P("dp", "vocab"),
        P("dp", "vocab"),
        P(None, "dp", "vocab", None, None),
        P(None, "dp", "vocab", None, None),
        P("dp", None),
        P("dp", None, None),
        P("vocab", None),
        P(),
        P(None, ("dp", "vocab")),
        P(),
    )
    out_specs = P("dp", None)
    return jax.shard_map(local, mesh=mesh, in_specs=in_specs, out_specs=out_specs, check_vma=False)
```

time: 787 us -> 204 us (0.26)
  waiting for transfers between devices: 575 us -> 0 us
  Pallas kernels: 0 us -> 177 us
  blocking collectives: 63.7 us -> 0 us
  local copies, waits for them, and re-layouts: 48.4 us -> 6.46 us
  matrix products: 50.1 us -> 15 us
  other arithmetic: 24.6 us -> 4.75 us
  between operations: 13.7 us -> 0.2 us
  starting transfers between devices: 7.91 us -> 0 us
    ppermute x6 -> x0, waiting for transfers between devices: 312 us -> none  [from_behind(): return lax.ppermute(block, axis, route)]
    pallas_call x0 -> x2, Pallas kernels: none -> 177 us  [the longest x1 135 us: local(): pl.pallas_call(functools.partial(tail_kernel, nd, nv, width), out_shape=j...]
    all_gather x1 -> x0, waiting for transfers between devices: 138 us -> none  [local(): lax.all_gather(normed_rows, 'dp', axis=0, tiled=True)]
    unnamed x3 -> x0, waiting for transfers between devices: 126 us -> none
    psum x1 -> x0, blocking collectives: 63.7 us -> none  [local(): hidden = lax.psum(placed, 'vocab').astype(jnp.bfloat16)]
    dot_general x4 -> x1, matrix products: 50.1 us -> 15 us  [local(): partial = jnp.dot(attended, out_weight, preferred_element_type=F32)]
    unnamed x38 -> x12, local copies, waits for them, and re-layouts: 35.4 us -> 4.97 us
    another operation x7 -> x0, other arithmetic: 8.33 us -> none  [the longest x6 7.75 us: local(): jnp.stack([cache_k[answer], cache_v[answer]])]
  transfers between devices with their start and end apart: 8 -> 0, of which waited for: 6 -> 0; matrix products, arithmetic and copies ran while one was open for 4% -> 0% of each run, Pallas kernels for 0% -> 0%
where the time goes in v1:
time: 204 us; the launch traced here: 203 us
  Pallas kernels  177 us (87%)
  matrix products  15 us (7%)
  local copies, waits for them, and re-layouts  6.46 us (3%)
  other arithmetic  4.75 us (2%)
    pallas_call x1, Pallas kernels, local(): pl.pallas_call(functools.partial(tail_kernel, nd, nv, width), out_shape=j...  135 us
    pallas_call x1, Pallas kernels, local(): pl.pallas_call(functools.partial(attend_kernel, nd), out_shape=jax.ShapeD...  41.6 us
    dot_general x1, matrix products, local(): partial = jnp.dot(attended, out_weight, preferred_element_type=F32)  15 us
    unnamed x12, local copies, waits for them, and re-layouts  4.97 us

profile of v1, /device:TPU:0, one launch (start us, length us, event | category | flops | bytes accessed | tf_op | source)
XLA Modules:
  0.0 203.4 jit_solution(14354544086266665537)
XLA Ops:
  0.0 0.0 copy-start.2
  0.0 0.7 copy.29
  0.8 2.6 %convert_reduce_fusion = s32[4,7,21]{0,2,1:T(8,128)S(1)} fusion(pred[21,21]{1,0:T(8,128)(4,1)S(1)} %iota_compare_fusion.4, pred[4,7,21]{2,0,1:T(4,128)(4,1)S(1)} %fusion.5), kind=kLoop, calls=%fused_computation.11 | loop fusion | flops 36456 | bytes 3381 | tf_op jit(solution)/shard_map/reduce_sum | solution.py:312
  3.3 0.1 copy.31
  3.5 0.7 multiply_add_fusion
  4.2 0.1 broadcast_in_dim.22
  4.3 0.1 reshape.49
  4.4 0.1 add.29
  4.5 0.1 pad_add_fusion
  4.6 0.3 fusion.place_ref
  4.8 0.4 fusion.2.pick_ref
  5.3 1.0 copy.40
  6.3 0.1 copy.46
  6.4 0.0 copy-done.2
  6.5 0.1 copy.39
  6.6 0.1 broadcast_in_dim.23.lens_ref
  6.6 0.0 copy-start
  6.6 3.1 %copy-done = bf16[7,4,2,512,128]{4,3,2,1,0:T(8,128)(2,1)S(1)} copy-done((bf16[7,4,2,512,128]{4,3,2,1,0:T(8,128)(2,1)S(1)}, bf16[7,4,2,512,128]{4,3,2,1,0:T(8,128)(2,1)}, u32[]{:S(2)}) %copy-start) | copy-done | bytes 7340056
  9.7 41.6 %shard_map.100 = bf16[4,2,176,128]{3,2,1,0:T(8,128)(2,1)S(1)} custom-call(bf16[4,336,176]{2,1,0:T(8,128)(2,1)S(1)} %fusion.2.pick_ref, bf16[4,352,336]{2,1,0:T(8,128)(2,1)S(1)} %fusion.place_ref, bf16[4,2,176,128]{3,2,1,0:T(8,128)(2,1)S(1)} %pad.24.q_ref, s32[7,8,128]{2,1,0:T(8,128)S(1)} %broadcast_in_dim.23.lens_ref, ...), custom_call_target="tpu_custom_call" | custom-call | tf_op jit(solution)/shard_map/pallas_call | solution.py:346
  51.3 0.1 copy_bitcast_fusion
  51.4 0.2 reshape.53
  51.5 0.0 copy-start.1
  51.6 0.0 copy-start.3
  51.6 15.0 %fusion.3.part_ref = f32[96,8192]{1,0:T(8,128)} fusion(bf16[2048,8192]{1,0:T(8,128)(2,1)} %param.16, bf16[84,2048]{1,0:T(8,128)(2,1)S(1)} %reshape.53), kind=kOutput, calls=%fused_computation.6 | convolution fusion | flops 3221225472 | bytes 37044224 | tf_op jit(solution)/shard_map/dot_general | solution.py:371
  66.6 0.7 dynamic-slice_convert_fusion
  67.3 0.0 copy-done.1
  67.3 0.0 copy-done.3
  67.4 0.1 broadcast_in_dim.25.ids_ref
  67.4 135.4 %shard_map.101 = f32[8,128]{1,0:T(8,128)S(1)} custom-call(f32[96,8192]{1,0:T(8,128)} %fusion.3.part_ref, bf16[96,2048]{1,0:T(8,128)(2,1)S(1)} %pad.27.res_ref, f32[8,2048]{1,0:T(8,128)S(1)} %broadcast_in_dim.24.gain_ref, bf16[4,2048,256]{2,1,0:T(8,128)(2,1)} %bitcast.29, s32[8,128]{1,0:T(8,128)S(1)} %broadcast_in_dim.25.ids_ref), custom_call_target="tpu_custom_call" | custom-call | tf_op jit(solution)/shard_map/pallas_call | solution.py:379
  202.9 0.6 slice_bitcast_fusion.1
  (15 shorter events, 0.2 us)
Async XLA Ops:
  0.0 6.4 %copy-start.2 = (s32[4,7]{1,0:T(4,128)S(1)}, s32[4,7]{1,0:T(4,128)}, u32[]{:S(2)}) copy-start(s32[4,7]{1,0:T(4,128)} %param.14) | copy-start | bytes 340
  6.6 3.1 %copy-start = (bf16[7,4,2,512,128]{4,3,2,1,0:T(8,128)(2,1)S(1)}, bf16[7,4,2,512,128]{4,3,2,1,0:T(8,128)(2,1)}, u32[]{:S(2)}) copy-start(bf16[7,4,2,512,128]{4,3,2,1,0:T(8,128)(2,1)} %k_hbm.1) | copy-start | bytes 22020100
  51.5 15.8 %copy-start.1 = (bf16[84,2048]{1,0:T(8,128)(2,1)S(1)}, bf16[84,2048]{1,0:T(8,128)(2,1)}, u32[]{:S(2)}) copy-start(bf16[84,2048]{1,0:T(8,128)(2,1)} %param.11) | copy-start | bytes 1032196
  51.6 15.8 %copy-start.3 = (s32[2]{0:T(128)S(1)}, s32[2]{0:T(128)}, u32[]{:S(2)}) copy-start(s32[2]{0:T(128)} %param.19) | copy-start | bytes 28

commit v2 on v1

--- a/solution.py
+++ b/solution.py
@@ -11,6 +11,7 @@
 MESH = pl.DeviceIdType.MESH
 F32 = jnp.float32
 BF16 = jnp.bfloat16
+BUFS = 4
 
 
 def up(n, m):
@@ -89,7 +90,10 @@
                 top = jnp.max(s, axis=1, keepdims=True)
                 e = jnp.exp(s - top)
                 total = jnp.sum(e, axis=1, keepdims=True)
-                o = jnp.dot(e.astype(BF16), v_ref[i, p, c], preferred_element_type=F32)
+                big = e.astype(BF16)
+                small = (e - big.astype(F32)).astype(BF16)
+                o = jnp.dot(big, v_ref[i, p, c], preferred_element_type=F32)
+                o = o + jnp.dot(small, v_ref[i, p, c], preferred_element_type=F32)
                 o = (o / total).astype(BF16)
                 if i:
                     ob[i, p, c] = o
@@ -112,7 +116,9 @@
     for i in order:
         o_out[i].wait_recv()
         s_out[i].wait_recv()
-    half = out_ref.shape[2]
+    half = place_ref.shape[1] // 2
+    group = out_ref.shape[1] // heads // hd
+    each = half // group
     for p in range(prompts):
         place = place_ref[p]
         both = jnp.dot(place, strecv[...], preferred_element_type=F32)
@@ -124,39 +130,74 @@
             first, second = jnp.exp(first - top), jnp.exp(second - top)
             o = jnp.dot(place, orecv[p, c], preferred_element_type=F32)
             mixed = (first * o[:half] + second * o[half:]) / (first + second)
-            out_ref[p, c] = mixed.astype(BF16)
+            mixed = mixed.astype(BF16)
+            for j in range(group):
+                at = (c * group + j) * hd
+                out_ref[p * each : (p + 1) * each, at : at + hd] = (
+                    mixed[j * each : (j + 1) * each])
     for i in order:
         for copy in (q_out[i], l_out[i], o_out[i], s_out[i]):
             copy.wait_send()
 
 
 def tail_kernel(
-    nd, nv, width, part_ref, res_ref, gain_ref, w_ref, ids_ref, out_ref,
-    sb, rb, hid, sq, sqr, g, stat, statr, vrow,
-    p_send, p_recv, q_send, q_recv, g_send, g_recv, t_send, t_recv, v_send, v_recv,
+    nd, nv, width, chunk, att_ref, ow_hbm, res_ref, gain_ref, w_ref, ids_ref, out_ref,
+    wb, own, sb, rb, hid, sq, sqr, g, stat, statr, vrow,
+    w_sem, p_send, p_recv, q_send, q_recv, g_send, g_recv, t_send, t_recv, v_send, v_recv,
 ):
     rows, share = res_ref.shape
     me, col = lax.axis_index("dp"), lax.axis_index("vocab")
-    vpeer = {j: lax.rem(col + j, nv) for j in range(1, nv)}
+    square = nv == 4
+    if square:
+        vpeer = {
+            3: 3 - col, 1: col + 1 - 2 * lax.rem(col, 2), 2: lax.rem(col + 2, nv)}
+    else:
+        vpeer = {j: lax.rem(col + j, nv) for j in range(1, nv)}
     dpeer = {j: lax.rem(me + j, nd) for j in range(1, nd)}
+    per = share // chunk
+    todo = [(j, t) for j in [*vpeer, 0] for t in range(per)]
+
+    def load(at):
+        j, t = todo[at]
+        v = vpeer[j] if j else col
+        start = pl.multiple_of(v * share + t * chunk, 128)
+        return pltpu.make_async_copy(
+            ow_hbm.at[:, pl.ds(start, chunk)], wb.at[at % BUFS], w_sem.at[at % BUFS])
+
+    for at in range(min(BUFS, len(todo))):
+        load(at).start()
     greet([(me, vpeer[j]) for j in vpeer] + [(dpeer[j], col) for j in dpeer])
-
-    def columns(v):
-        return pl.ds(pl.multiple_of(v * share, 128), share)
-
+    step = 256 if chunk % 256 == 0 else 128
     parts = {}
-    for j in vpeer:
-        sb[j] = part_ref[:, columns(vpeer[j])].astype(BF16)
-        parts[j] = remote(
-            sb.at[j], rb.at[j], p_send.at[j], p_recv.at[j], (me, vpeer[j]))
-        parts[j].start()
-    for j in vpeer:
-        parts[j].wait_recv()
-    step = 256 if share % 256 == 0 else 128
+    for at, (j, t) in enumerate(todo):
+        load(at).wait()
+
+        def tile(u, carry, at=at, j=j, t=t):
+            here = pl.ds(pl.multiple_of(u * step, step), step)
+            there = pl.ds(pl.multiple_of(t * chunk + u * step, step), step)
+            got = jnp.dot(
+                att_ref[...], wb[at % BUFS, :, here], preferred_element_type=F32)
+            if j:
+                sb[j, :, there] = got.astype(BF16)
+            else:
+                own[:, there] = got + res_ref[:, there].astype(F32)
+            return carry
+
+        lax.fori_loop(0, chunk // step, tile, 0)
+        if at + BUFS < len(todo):
+            load(at + BUFS).start()
+        if j:
+            there = pl.ds(t * chunk, chunk)
+            parts[j, t] = remote(
+                sb.at[j, :, there], rb.at[j, :, there],
+                p_send.at[j, t], p_recv.at[j, t], (me, vpeer[j]))
+            parts[j, t].start()
     squares = jnp.zeros((rows, 128), F32)
     for t in range(0, share, step):
-        total = part_ref[:, pl.ds(pl.multiple_of(col * share + t, 128), step)]
-        total = total + res_ref[:, t : t + step].astype(F32)
+        if t % chunk == 0:
+            for j in vpeer:
+                parts[j, t // chunk].wait_recv()
+        total = own[:, t : t + step]
         for j in vpeer:
             total = total + rb[j, :, t : t + step].astype(F32)
         total = total.astype(BF16)
@@ -196,23 +237,42 @@
         remote(block, block, g_send.at[0], g_recv.at[e, v], (sib, col)).wait_recv()
 
     nz = nd // 2
-    lines = [lax.rem(me + 2 * s, nd) for s in range(nz)]
-    slot = 0
-    for s in range(1, nz):
-        push(me, col, (lines[s], col), slot)
-        slot += 1
-    for j in vpeer:
-        push(me, col, (me, vpeer[j]), slot)
-        slot += 1
-    push(me, col, (sib, col), slot)
-    slot += 1
-    for s in range(1, nz):
-        arrived(lines[s], col)
-        for j in vpeer:
-            push(lines[s], col, (me, vpeer[j]), slot)
-            slot += 1
-        push(lines[s], col, (sib, col), slot)
-        slot += 1
+    z = lax.div(me, 2)
+    upper = lax.div(z, nz // 2)
+    mirrored = z + upper * (nz - 1 - 2 * z)
+    lines = [me]
+    for t in range(nz - 1):
+        at = t + lax.div(t - mirrored + nz, nz)
+        lines.append(2 * (at + upper * (nz - 1 - 2 * at)) + core)
+    slot = [0]
+
+    def send(e, v, device):
+        push(e, v, device, slot[0])
+        slot[0] += 1
+
+    direct = [1, 2] if square else list(vpeer)
+
+    def spread(s):
+        e = lines[s]
+        if s:
+            arrived(e, col)
+        for j in direct:
+            send(e, col, (me, vpeer[j]))
+        if s == 0:
+            for t in reversed(range(1, nz)):
+                send(e, col, (lines[t], col))
+        send(e, col, (sib, col))
+
+    def collect(s):
+        e = lines[s]
+        for j in direct:
+            arrived(e, vpeer[j])
+            if square and j == 1 + s % 2:
+                send(e, vpeer[j], (me, vpeer[3 - j]))
+            send(e, vpeer[j], (sib, col))
+        if square:
+            arrived(e, vpeer[3])
+            send(e, vpeer[3], (sib, col))
 
     base = (me * nv + col) * width
     cols = lax.broadcasted_iota(jnp.int32, (rows, width), 1) + base
@@ -235,11 +295,6 @@
             tile = jnp.concatenate([tile, tail], axis=0)
         stat[e] = jnp.transpose(tile)[0:8]
 
-    for s in range(nz):
-        for j in vpeer:
-            arrived(lines[s], vpeer[j])
-            push(lines[s], vpeer[j], (sib, col), slot)
-            slot += 1
     stats = []
 
     def deliver(e, at):
@@ -248,16 +303,23 @@
         copy.start()
         stats.append(copy)
 
-    for s in range(nz):
-        head(lines[s])
-        if s:
-            deliver(lines[s], 2 * s)
-    for s in range(nz):
-        other = lax.rem(sib + 2 * s, nd)
+    def finish(s):
+        other = lines[s] + 1 - 2 * core
         for v in range(nv):
             arrived(other, v)
         head(other)
         deliver(other, 2 * s + 1)
+
+    spread(0)
+    for s in range(nz):
+        if s + 1 < nz:
+            spread(s + 1)
+        collect(s)
+        head(lines[s])
+        if s:
+            deliver(lines[s], 2 * s)
+            finish(s - 1)
+    finish(nz - 1)
     statr[me] = stat[me]
     for j in dpeer:
         e = dpeer[j]
@@ -303,7 +365,7 @@
     return pltpu.SemaphoreType.DMA(shape)
 
 
-def selectors(pairs, answers, group, span, slots):
+def selectors(pairs, answers, group, span, slots, each):
     prompts, per_prompt, _ = pairs.shape
     ids = jnp.arange(answers, dtype=jnp.int32)
     chosen = pairs[:, None, :, :] == ids[None, :, None, None]
@@ -319,7 +381,11 @@
     row = jnp.arange(answers * span, dtype=jnp.int32)
     first, second = wide[:, :, 0], wide[:, :, 1]
     pick = (row[None, :, None] == first[:, None, :]) | (row[None, :, None] == second[:, None, :])
-    both = jnp.concatenate([first, second], axis=1)
+    both = jnp.pad(
+        key, ((0, 0), (0, each - per_prompt), (0, 0)), constant_values=-group)
+    both = both.transpose(0, 2, 1)[:, :, None, :] + jnp.arange(
+        group, dtype=jnp.int32)[None, None, :, None]
+    both = both.reshape(prompts, 2 * group * each)
     place = both[:, :, None] == row[None, None, :]
     return pick.astype(BF16), place.astype(BF16)
 
@@ -335,7 +401,9 @@
     group = queries.shape[1] // hd // heads
     span = up((answers - 1) * group, 16)
     slots = up(per_prompt * group, 16)
-    pick, place = selectors(pairs, answers, group, span, slots)
+    each = up(per_prompt, 8)
+    rows = prompts * each
+    pick, place = selectors(pairs, answers, group, span, slots, each)
     q = queries.reshape(prompts, per_prompt, heads, group, hd).transpose(0, 2, 1, 3, 4)
     q = q.reshape(prompts, heads, per_prompt * group, hd)
     q = jnp.pad(q, ((0, 0), (0, 0), (0, slots - per_prompt * group), (0, 0)))
@@ -345,7 +413,7 @@
     hbm = pl.BlockSpec(memory_space=pl.ANY)
     attended = pl.pallas_call(
         functools.partial(attend_kernel, nd),
-        out_shape=jax.ShapeDtypeStruct((prompts, heads, slots, hd), BF16),
+        out_shape=jax.ShapeDtypeStruct((rows, queries.shape[1]), BF16),
         in_specs=[vm, vm, vm, vm, hbm, hbm],
         out_specs=vm,
         scratch_shapes=[
@@ -361,27 +429,26 @@
             dma(2, answers),
         ] + [dma(answers)] * 8,
         compiler_params=pltpu.CompilerParams(
-            collective_id=0, has_side_effects=True, vmem_limit_bytes=40 << 20),
+            collective_id=0, has_side_effects=True, vmem_limit_bytes=56 << 20),
     )(pick, place, q, lens, cache_k, cache_v)
-    attended = attended[:, :, : per_prompt * group].reshape(
-        prompts, heads, per_prompt, group, hd).transpose(0, 2, 1, 3, 4)
-    rows = up(pair_rows, 16)
-    attended = jnp.pad(
-        attended.reshape(pair_rows, heads * group * hd), ((0, rows - pair_rows), (0, 0)))
-    partial = jnp.dot(attended, out_weight, preferred_element_type=F32)
     share = residual.shape[1]
     width = head_weight.shape[1]
-    res = jnp.pad(residual, ((0, rows - pair_rows), (0, 0)))
+    res = jnp.pad(
+        residual.reshape(prompts, per_prompt, share),
+        ((0, 0), (0, each - per_prompt), (0, 0))).reshape(rows, share)
+    chunk = min(share, 1024)
     own_gain = lax.dynamic_slice_in_dim(norm_gain, lax.axis_index("vocab") * share, share, 0)
     own_gain = jnp.broadcast_to(own_gain.astype(F32)[None], (8, share))
     ids = jnp.broadcast_to(jnp.pad(answer_ids, (0, 6))[:, None], (8, 128))
     wide = up(rows, 128)
     verdict = pl.pallas_call(
-        functools.partial(tail_kernel, nd, nv, width),
+        functools.partial(tail_kernel, nd, nv, width, chunk),
         out_shape=jax.ShapeDtypeStruct((8, wide), F32),
-        in_specs=[vm] * 5,
+        in_specs=[vm, hbm] + [vm] * 4,
         out_specs=vm,
         scratch_shapes=[
+            pltpu.VMEM((BUFS, attended.shape[1], chunk), BF16),
+            pltpu.VMEM((rows, share), F32),
             pltpu.VMEM((nv, rows, share), BF16),
             pltpu.VMEM((nv, rows, share), BF16),
             pltpu.VMEM((rows, share), BF16),
@@ -391,14 +458,15 @@
             pltpu.VMEM((nd, 8, wide), F32),
             pltpu.VMEM((nd, 8, wide), F32),
             pltpu.VMEM((nv, 8, wide), F32),
-            dma(nv), dma(nv), dma(nv), dma(nv),
+            dma(BUFS), dma(nv, share // chunk), dma(nv, share // chunk), dma(nv), dma(nv),
             dma((nd // 2) * (2 * nv + 1)), dma(nd, nv),
             dma(nd), dma(nd), dma(nv), dma(nv),
         ],
         compiler_params=pltpu.CompilerParams(
             collective_id=1, has_side_effects=True, vmem_limit_bytes=52 << 20),
-    )(partial, res, own_gain, head_weight.reshape(nv, share, width), ids)
-    return verdict[:2, :pair_rows].T
+    )(attended, out_weight, res, own_gain, head_weight.reshape(nv, share, width), ids)
+    verdict = verdict[:2, :rows].reshape(2, prompts, each)[:, :, :per_prompt]
+    return verdict.reshape(2, pair_rows).T
 
 
 def solution(mesh):

time: 204 us -> 190 us (0.931)
  matrix products: 15 us -> 0 us
    dot_general x1 -> x0, matrix products: 15 us -> none  [local(): partial = jnp.dot(attended, out_weight, preferred_element_type=F32)]
    pallas_call x1, Pallas kernels: 135 us -> 132 us  [local(): pl.pallas_call(functools.partial(tail_kernel, nd, nv, width, chunk), out_...]
    unnamed x12 -> x15, local copies, waits for them, and re-layouts: 4.97 us -> 1.93 us
    pallas_call x1, Pallas kernels: 41.6 us -> 43.7 us  [local(): pl.pallas_call(functools.partial(attend_kernel, nd), out_shape=jax.ShapeD...]
where the time goes in v2:
time: 190 us; the launch traced here: 187 us
  Pallas kernels  176 us (93%)
  other arithmetic  6.58 us (3%)
  local copies, waits for them, and re-layouts  5 us (3%)
    pallas_call x1, Pallas kernels, local(): pl.pallas_call(functools.partial(tail_kernel, nd, nv, width, chunk), out_...  132 us
    pallas_call x1, Pallas kernels, local(): pl.pallas_call(functools.partial(attend_kernel, nd), out_shape=jax.ShapeD...  43.7 us

profile of v2, /device:TPU:0, one launch (start us, length us, event | category | flops | bytes accessed | tf_op | source)
XLA Modules:
  0.0 187.4 jit_solution(13774690827620251628)
XLA Ops:
  0.0 0.0 copy-start.1
  0.0 0.7 copy.26
  0.8 2.6 %convert_reduce_fusion = s32[4,7,21]{0,2,1:T(8,128)S(1)} fusion(pred[21,21]{1,0:T(8,128)(4,1)S(1)} %iota_compare_fusion.4, pred[4,7,21]{2,0,1:T(4,128)(4,1)S(1)} %fusion.3), kind=kLoop, calls=%fused_computation.7 | loop fusion | flops 36456 | bytes 3381 | tf_op jit(solution)/shard_map/reduce_sum | solution.py:374
  3.4 0.1 copy.28
  3.5 0.7 multiply_add_fusion
  4.2 0.1 broadcast_in_dim.22
  4.3 0.1 reshape.69
  4.4 0.1 add.52
  4.5 0.0 copy-start.3
  4.6 1.3 fusion.2.pick_ref
  5.9 0.1 add.56
  6.0 0.1 add.58
  6.1 1.3 fusion.place_ref
  7.3 0.0 copy-done.1
  7.3 0.1 copy.36
  7.4 0.1 copy.41
  7.5 0.8 pad.26.q_ref
  8.3 0.0 copy-done.3
  8.3 0.1 copy.35
  8.4 0.7 broadcast_in_dim.23.lens_ref
  9.1 0.0 copy-start.2
  9.1 0.0 copy-start.4
  9.1 43.7 %shard_map.100.att_ref = bf16[96,2048]{1,0:T(8,128)(2,1)} custom-call(bf16[4,336,176]{2,1,0:T(8,128)(2,1)} %fusion.2.pick_ref, bf16[4,384,336]{2,1,0:T(8,128)(2,1)} %fusion.place_ref, bf16[4,2,176,128]{3,2,1,0:T(8,128)(2,1)} %pad.26.q_ref, s32[7,8,128]{2,1,0:T(8,128)} %broadcast_in_dim.23.lens_ref, bf16[7,4,2,512,128]{4,3,2,1,0:T(8,128)(2,1)} %k_hbm.1, ...), custom_call_target="tpu_custom_call" | custom-call | tf_op jit(solution)/shard_map/pallas_call | solution.py:414
  52.8 0.7 dynamic-slice_convert_fusion
  53.5 0.0 copy-done.2
  53.5 0.1 reshape.72
  53.6 0.0 copy-done.4
  53.6 0.1 broadcast_in_dim.25.ids_ref
  53.7 0.0 copy-start
  53.7 1.0 copy-done
  54.7 131.9 %shard_map.101 = f32[8,128]{1,0:T(8,128)S(1)} custom-call(bf16[96,2048]{1,0:T(8,128)(2,1)S(1)} %copy-done, bf16[2048,8192]{1,0:T(8,128)(2,1)} %ow_hbm.1, bf16[96,2048]{1,0:T(8,128)(2,1)S(1)} %bitcast.26, f32[8,2048]{1,0:T(8,128)S(1)} %broadcast_in_dim.24.gain_ref, bf16[4,2048,256]{2,1,0:T(8,128)(2,1)} %bitcast.27, s32[8,128]{1,0:T(8,128)S(1)} %broadcast_in_dim.25.ids_ref), custom_call_target="tpu_custom_call" | custom-call | tf_op jit(solution)/shard_map/pallas_call | solution.py:444
  186.7 0.1 reshape.75
  186.7 0.6 reshape.76
  (20 shorter events, 0.2 us)
Async XLA Ops:
  0.0 7.3 %copy-start.1 = (bf16[84,2048]{1,0:T(8,128)(2,1)S(1)}, bf16[84,2048]{1,0:T(8,128)(2,1)}, u32[]{:S(2)}) copy-start(bf16[84,2048]{1,0:T(8,128)(2,1)} %param.10) | copy-start | bytes 1032196
  4.5 3.7 %copy-start.3 = (s32[4,7]{1,0:T(4,128)S(1)}, s32[4,7]{1,0:T(4,128)}, u32[]{:S(2)}) copy-start(s32[4,7]{1,0:T(4,128)} %param.14) | copy-start | bytes 340
  9.1 44.4 %copy-start.2 = (bf16[84,2048]{1,0:T(8,128)(2,1)S(1)}, bf16[84,2048]{1,0:T(8,128)(2,1)}, u32[]{:S(2)}) copy-start(bf16[84,2048]{1,0:T(8,128)(2,1)} %param.11) | copy-start | bytes 1032196
  9.1 44.6 %copy-start.4 = (s32[2]{0:T(128)S(1)}, s32[2]{0:T(128)}, u32[]{:S(2)}) copy-start(s32[2]{0:T(128)} %param.19) | copy-start | bytes 28
  53.7 1.0 copy-start

commit v3 on v2

--- a/solution.py
+++ b/solution.py
@@ -279,21 +279,26 @@
     lane = lax.broadcasted_iota(jnp.int32, (rows, 128), 1)
     tail = jnp.zeros((128 - rows % 128, 128), F32) if rows % 128 else None
 
-    def head(e):
+    def head(start):
         def body(v, acc):
-            return acc + jnp.dot(g[e, v], w_ref[v], preferred_element_type=F32)
-
-        logits = lax.fori_loop(0, nv, body, jnp.zeros((rows, width), F32))
-        top = jnp.max(logits, axis=1, keepdims=True)
-        total = jnp.sum(jnp.exp(logits - top), axis=1, keepdims=True)
-        yes = jnp.sum(jnp.where(cols == ids_ref[0:1, 0:1], logits, 0.0), axis=1, keepdims=True)
-        no = jnp.sum(jnp.where(cols == ids_ref[1:2, 0:1], logits, 0.0), axis=1, keepdims=True)
-        tile = jnp.where(lane == 0, top, 0.0)
-        for at, what in ((1, total), (2, yes), (3, no)):
-            tile = jnp.where(lane == at, what, tile)
-        if tail is not None:
-            tile = jnp.concatenate([tile, tail], axis=0)
-        stat[e] = jnp.transpose(tile)[0:8]
+            block = g[pl.ds(start, 2), v].reshape(2 * rows, share)
+            return acc + jnp.dot(block, w_ref[v], preferred_element_type=F32)
+
+        both = lax.fori_loop(0, nv, body, jnp.zeros((2 * rows, width), F32))
+        for half in range(2):
+            logits = both[half * rows : (half + 1) * rows]
+            top = jnp.max(logits, axis=1, keepdims=True)
+            total = jnp.sum(jnp.exp(logits - top), axis=1, keepdims=True)
+            yes = jnp.sum(
+                jnp.where(cols == ids_ref[0:1, 0:1], logits, 0.0), axis=1, keepdims=True)
+            no = jnp.sum(
+                jnp.where(cols == ids_ref[1:2, 0:1], logits, 0.0), axis=1, keepdims=True)
+            tile = jnp.where(lane == 0, top, 0.0)
+            for at, what in ((1, total), (2, yes), (3, no)):
+                tile = jnp.where(lane == at, what, tile)
+            if tail is not None:
+                tile = jnp.concatenate([tile, tail], axis=0)
+            stat[start + half] = jnp.transpose(tile)[0:8]
 
     stats = []
 
@@ -307,7 +312,9 @@
         other = lines[s] + 1 - 2 * core
         for v in range(nv):
             arrived(other, v)
-        head(other)
+        head(lines[s] - core)
+        if s:
+            deliver(lines[s], 2 * s)
         deliver(other, 2 * s + 1)
 
     spread(0)
@@ -315,9 +322,7 @@
         if s + 1 < nz:
             spread(s + 1)
         collect(s)
-        head(lines[s])
         if s:
-            deliver(lines[s], 2 * s)
             finish(s - 1)
     finish(nz - 1)
     statr[me] = stat[me]

time: 190 us -> 187 us (0.984)
  Pallas kernels: 176 us -> 172 us
    pallas_call x1, Pallas kernels: 132 us -> 128 us  [local(): pl.pallas_call(functools.partial(tail_kernel, nd, nv, width, chunk), out_...]
where the time goes in v3:
time: 187 us; the launch traced here: 184 us
  Pallas kernels  172 us (92%)
  other arithmetic  6.58 us (4%)
  local copies, waits for them, and re-layouts  5 us (3%)
    pallas_call x1, Pallas kernels, local(): pl.pallas_call(functools.partial(tail_kernel, nd, nv, width, chunk), out_...  128 us
    pallas_call x1, Pallas kernels, local(): pl.pallas_call(functools.partial(attend_kernel, nd), out_shape=jax.ShapeD...  43.7 us

profile of v3, /device:TPU:0, one launch (start us, length us, event | category | flops | bytes accessed | tf_op | source)
XLA Modules:
  0.0 183.8 jit_solution(2633582669093863262)
XLA Ops:
  0.0 0.0 copy-start.1
  0.0 0.7 copy.26
  0.8 2.6 %convert_reduce_fusion = s32[4,7,21]{0,2,1:T(8,128)S(1)} fusion(pred[21,21]{1,0:T(8,128)(4,1)S(1)} %iota_compare_fusion.4, pred[4,7,21]{2,0,1:T(4,128)(4,1)S(1)} %fusion.3), kind=kLoop, calls=%fused_computation.7 | loop fusion | flops 36456 | bytes 3381 | tf_op jit(solution)/shard_map/reduce_sum | solution.py:379
  3.4 0.1 copy.28
  3.5 0.7 multiply_add_fusion
  4.2 0.1 broadcast_in_dim.22
  4.3 0.1 reshape.69
  4.4 0.1 add.52
  4.5 0.0 copy-start.3
  4.6 1.3 fusion.2.pick_ref
  5.9 0.1 add.56
  6.0 0.1 add.58
  6.1 1.3 fusion.place_ref
  7.3 0.0 copy-done.1
  7.3 0.1 copy.36
  7.4 0.1 copy.41
  7.5 0.8 pad.26.q_ref
  8.3 0.0 copy-done.3
  8.3 0.1 copy.35
  8.4 0.7 broadcast_in_dim.23.lens_ref
  9.1 0.0 copy-start.2
  9.1 0.0 copy-start.4
  9.1 43.7 %shard_map.100.att_ref = bf16[96,2048]{1,0:T(8,128)(2,1)} custom-call(bf16[4,336,176]{2,1,0:T(8,128)(2,1)} %fusion.2.pick_ref, bf16[4,384,336]{2,1,0:T(8,128)(2,1)} %fusion.place_ref, bf16[4,2,176,128]{3,2,1,0:T(8,128)(2,1)} %pad.26.q_ref, s32[7,8,128]{2,1,0:T(8,128)} %broadcast_in_dim.23.lens_ref, bf16[7,4,2,512,128]{4,3,2,1,0:T(8,128)(2,1)} %k_hbm.1, ...), custom_call_target="tpu_custom_call" | custom-call | tf_op jit(solution)/shard_map/pallas_call | solution.py:419
  52.8 0.7 dynamic-slice_convert_fusion
  53.5 0.0 copy-done.2
  53.5 0.1 reshape.72
  53.6 0.0 copy-done.4
  53.6 0.1 broadcast_in_dim.25.ids_ref
  53.7 0.0 copy-start
  53.7 1.0 copy-done
  54.7 128.3 %shard_map.101 = f32[8,128]{1,0:T(8,128)S(1)} custom-call(bf16[96,2048]{1,0:T(8,128)(2,1)S(1)} %copy-done, bf16[2048,8192]{1,0:T(8,128)(2,1)} %ow_hbm.1, bf16[96,2048]{1,0:T(8,128)(2,1)S(1)} %bitcast.26, f32[8,2048]{1,0:T(8,128)S(1)} %broadcast_in_dim.24.gain_ref, bf16[4,2048,256]{2,1,0:T(8,128)(2,1)} %bitcast.27, s32[8,128]{1,0:T(8,128)S(1)} %broadcast_in_dim.25.ids_ref), custom_call_target="tpu_custom_call" | custom-call | tf_op jit(solution)/shard_map/pallas_call | solution.py:449
  183.1 0.1 reshape.75
  183.1 0.6 reshape.76
  (20 shorter events, 0.2 us)
Async XLA Ops:
  0.0 7.3 %copy-start.1 = (bf16[84,2048]{1,0:T(8,128)(2,1)S(1)}, bf16[84,2048]{1,0:T(8,128)(2,1)}, u32[]{:S(2)}) copy-start(bf16[84,2048]{1,0:T(8,128)(2,1)} %param.10) | copy-start | bytes 1032196
  4.5 3.7 %copy-start.3 = (s32[4,7]{1,0:T(4,128)S(1)}, s32[4,7]{1,0:T(4,128)}, u32[]{:S(2)}) copy-start(s32[4,7]{1,0:T(4,128)} %param.14) | copy-start | bytes 340
  9.1 44.4 %copy-start.2 = (bf16[84,2048]{1,0:T(8,128)(2,1)S(1)}, bf16[84,2048]{1,0:T(8,128)(2,1)}, u32[]{:S(2)}) copy-start(bf16[84,2048]{1,0:T(8,128)(2,1)} %param.11) | copy-start | bytes 1032196
  9.1 44.6 %copy-start.4 = (s32[2]{0:T(128)S(1)}, s32[2]{0:T(128)}, u32[]{:S(2)}) copy-start(s32[2]{0:T(128)} %param.19) | copy-start | bytes 28
  53.7 1.0 copy-start
